TPU v7x, 32 devices: a whole 2x2x4 slice. The times are simulated.
32 devices in a mesh: run: 2 (over y), area: 16 (over z, x, core).
Axes of the slice: x: 2, y: 2, z: 4, core: 2. Of those that a mesh axis runs over, the one named last changes fastest.
Arguments:
- pattern: int32 [2048, 128, 128], P('area'), may hold values from 0 to 1999
- target_area: int32 [2048, 1], replicated, may hold values from 0 to 15; in each aligned block of 128 rows (0 to 127, 128 to 255, ...) at most 16 rows name the same one
- source_block: int32 [2048], replicated, may hold values from 0 to 3
- target_block: int32 [2048], replicated, may hold values from 0 to 3
- neuron_lag: int32 [8192], replicated, may hold values from 0 to 15
- tau_mem: float32 [8192], P('area'), may hold values from 1 to 20
- v_init: float32 [16384], P(('run', 'area')), parts along dimension 0, may hold values from -4 to 4
- ext_count: int32 [10, 16384], P(None, ('run', 'area')), parts along dimension 1, may hold values from 0 to 3
Outputs:
- membrane: float32 [16384], P(('run', 'area')), parts along dimension 0
- activity: bfloat16 [10, 16384], P(None, ('run', 'area')), parts along dimension 1
- pending: float32 [15, 16384], P(None, ('run', 'area')), parts along dimension 1
There are 2 independent parts, one for each index of `run`. A program takes and returns all parts, laid end to end along the dimension named above; an argument that names none is the same for every part. Nothing has to cross between parts.
Inputs may be any that keep to these rules, and one draw needn't show every extreme that they name: `target_area`: among the 128 rows of one builder no area is named more than 16 times, a bound that some block reaches.
All inputs are finite; a program needn't handle non-finite values.
Results may differ from a plain program's by a relative error of at most 0.0038.
Values may be sent and summed in bfloat16 or wider, within the bound.
A program may use at most 128 MiB of HBM per device.

v0:
```python
import math

import jax
import jax.numpy as jnp
from jax import lax
from jax.sharding import PartitionSpec as P

BLK = 128
NB = 4
OUT_DEV = 128
DELAYS = 15
LAGS = 16


step_ms = 0.1
ext_gain = 0.25
threshold = 1.0
slope = 4.0
reset_part = 0.5
inhib_gain = 3.0


def block_weights(pattern_rows, source_rows):
    factor = 8.0 / math.sqrt(BLK * OUT_DEV / NB)
    magnitude = jnp.maximum(pattern_rows.astype(jnp.float32) - 999.0, 0.0) / 1000.0
    signs = jnp.where(source_rows == NB - 1, -inhib_gain, 1.0).astype(jnp.float32)
    return (factor * magnitude * signs[:, None, None]).astype(jnp.bfloat16)


def to_delays(q_lag, lag_target):
    classes = jnp.arange(LAGS, dtype=jnp.int32)
    target_slot = (classes[:, None] + 2 * lag_target[None, :]) % DELAYS
    hits = target_slot[None, :, :] == jnp.arange(DELAYS, dtype=jnp.int32)[:, None, None]
    return jnp.sum(jnp.where(hits, q_lag[None], jnp.zeros((), jnp.float32)), axis=1)


def lag_product(inputs, lags, weights):
    classes = jnp.arange(LAGS, dtype=jnp.int32)
    sorted_in = jnp.where(
        lags[:, None, :] == classes[None, :, None], inputs[:, None, :], jnp.zeros((), jnp.bfloat16)
    )
    return jnp.einsum("sci,sij->scj", sorted_in, weights, preferred_element_type=jnp.float32)


def collect(target_hot, terms):
    return jnp.einsum("sb,scj->bcj", target_hot, terms, precision=lax.Precision.HIGHEST)


def body(pattern, target_area, source_block, target_block, neuron_lag, tau_mem, v_init, ext_count):
    area_count = lax.axis_size("area")
    own_index = lax.axis_index("area")
    local_n = v_init.shape[0]
    block_count = local_n // BLK
    out_count = pattern.shape[0]
    capacity = max(2, 2 * out_count // area_count)
    slot_count = area_count * capacity
    step_count = ext_count.shape[0]
    route_all = target_area[:, 0].reshape(area_count, out_count)
    src_all = source_block.reshape(area_count, out_count)
    tgt_all = target_block.reshape(area_count, out_count)
    order = jnp.arange(out_count, dtype=jnp.int32)
    earlier = order[None, :] < order[:, None]
    same_route = route_all[:, :, None] == route_all[:, None, :]
    rank_all = jnp.sum((same_route & earlier[None]).astype(jnp.int32), axis=2)
    own_route = lax.dynamic_index_in_dim(route_all, own_index, 0, keepdims=False)
    own_rank = lax.dynamic_index_in_dim(rank_all, own_index, 0, keepdims=False)
    own_src = lax.dynamic_index_in_dim(src_all, own_index, 0, keepdims=False)
    destination = own_route * capacity + own_rank
    mine = route_all == own_index
    picks = (
        mine[:, :, None]
        & (rank_all[:, :, None] == jnp.arange(capacity, dtype=jnp.int32)[None, None, :])
    ).astype(jnp.int32)
    filled = jnp.sum(picks, axis=1).reshape(slot_count)
    slot_src = jnp.sum(picks * src_all[:, :, None], axis=1).reshape(slot_count)
    slot_tgt = jnp.sum(picks * tgt_all[:, :, None], axis=1).reshape(slot_count)
    slot_dev = jnp.arange(slot_count, dtype=jnp.int32) // capacity
    lag_rows = neuron_lag.reshape(area_count * block_count, BLK)
    slot_lag = lag_rows[slot_dev * block_count + slot_src]
    target_hot = (
        (slot_tgt[:, None] == jnp.arange(block_count, dtype=jnp.int32)[None, :])
        & (filled[:, None] > 0)
    ).astype(jnp.float32)
    own_lag = lax.dynamic_slice_in_dim(neuron_lag, own_index * local_n, local_n, 0)
    weights = block_weights(pattern, own_src)
    alpha = jnp.exp(-step_ms / tau_mem)
    outbox = jnp.zeros((slot_count, BLK, BLK), jnp.bfloat16).at[destination].set(weights)
    inbox = lax.all_to_all(
        outbox.reshape(area_count, capacity, BLK, BLK),
        "area",
        split_axis=0,
        concat_axis=0,
        tiled=True,
    )
    inbox = inbox.reshape(slot_count, BLK, BLK)
    due = jnp.zeros((DELAYS, local_n), jnp.float32)
    volt = v_init
    records = []
    for step in range(step_count):
        volt = alpha * volt + due[0] + ext_gain * (ext_count[step].astype(jnp.float32) - 1.5)
        rate = jax.nn.sigmoid(slope * (volt - threshold))
        volt = volt - reset_part * rate
        spikes = rate.astype(jnp.bfloat16)
        records.append(spikes)
        piece = lax.all_gather(spikes, "area", axis=0, tiled=True)
        count = piece.shape[0] // local_n
        span = count * capacity
        piece_rows = piece.reshape(count * block_count, BLK)
        inputs = piece_rows[jnp.arange(span, dtype=jnp.int32) // capacity * block_count + slot_src]
        q_sum = collect(target_hot, lag_product(inputs, slot_lag, inbox))
        q_lag = q_sum.transpose(1, 0, 2).reshape(LAGS, local_n)
        due = jnp.concatenate([due[1:], jnp.zeros((1, local_n), jnp.float32)], 0) + to_delays(
            q_lag, own_lag
        )
    return (volt, jnp.stack(records), due)


def solution(mesh):
    in_specs = (
        P("area", None, None),
        P(),
        P(),
        P(),
        P(),
        P("area"),
        P(("run", "area")),
        P(None, ("run", "area")),
    )
    out_specs = (P(("run", "area")), P(None, ("run", "area")), P(None, ("run", "area")))
    return jax.shard_map(body, mesh=mesh, in_specs=in_specs, out_specs=out_specs, check_vma=False)
```

profile of v0, /device:TPU:11, one launch (start us, length us, event | category | flops | bytes accessed | tf_op | source)
XLA Modules:
  0.0 472.2 jit_solution(6537822971238651789)
XLA Ops:
  0.7 1.4 convert_reduce_fusion
  3.5 6.7 %multiply_convert_fusion = bf16[128,128,128]{2,1,0:T(8,128)(2,1)} fusion(s32[128,128,128]{2,1,0:T(8,128)} %param.8, f32[128]{0:T(128)S(1)} %multiply_bitcast_fusion), kind=kLoop, calls=%fused_computation.12 | loop fusion | flops 10485760 | bytes 12583424 | tf_op jit(solution)/shard_map/convert_element_type | solution.py:27
  10.2 5.3 %broadcast_in_dim.255 = bf16[256,128,128]{2,1,0:T(8,128)(2,1)} broadcast(bf16[]{:T(256)} %constant.151.clone.1), dimensions={} | broadcast | bytes 8388610 | tf_op jit(solution)/shard_map/broadcast_in_dim | solution.py:87
  15.5 19.3 %scatter_fusion = bf16[256,128,128]{2,1,0:T(8,128)(2,1)} fusion(bf16[256,128,128]{2,1,0:T(8,128)(2,1)} %broadcast_in_dim.255, s32[128]{0:T(128)S(1)} %fusion.90, bf16[128,128,128]{2,1,0:T(8,128)(2,1)} %multiply_convert_fusion), kind=kCustom, calls=%fused_computation.11 | custom fusion | bytes 12583424 | tf_op jit(solution)/shard_map/scatter | solution.py:87
  34.9 6.7 %all-to-all-start = ((bf16[16,16,128,128]{3,2,1,0:T(8,128)(2,1)}), bf16[16,16,128,128]{3,2,1,0:T(8,128)(2,1)}, u32[]{:S(2)}, u32[]{:S(2)}) async-start(bf16[16,16,128,128]{3,2,1,0:T(8,128)(2,1)} %bitcast.104), calls=%async_computation | async-start | bytes 16777216 | tf_op jit(solution)/shard_map/all_to_all | solution.py:88
  41.8 0.9 select_reduce_fusion.10
  42.7 190.7 %all-gather = bf16[16,1,512]{2,1,0:T(2,128)(2,1)S(1)} all-gather(bf16[1,1,512]{2,1,0:T(2,128)(2,1)S(1)} %reshape.391), channel_id=1, replica_groups=mesh['run'=2,'area'=16] {'area'}, dimensions={0}, use_global_device_ids=true | all-gather | bytes 17408 | tf_op jit(solution)/shard_map/all_gather | solution.py:105
  233.6 0.9 gather_fusion.1
  234.4 0.7 gather_fusion
  235.5 4.7 fusion.30
  240.1 1.3 fusion.18
  241.6 15.1 %all-gather.1 = bf16[16,1,512]{2,1,0:T(2,128)(2,1)S(1)} all-gather(bf16[1,1,512]{2,1,0:T(2,128)(2,1)S(1)} %reshape.393), channel_id=1, replica_groups=mesh['run'=2,'area'=16] {'area'}, dimensions={0}, use_global_device_ids=true | all-gather | bytes 17408 | tf_op jit(solution)/shard_map/all_gather | solution.py:105
  256.9 0.9 gather_fusion.2
  257.7 4.7 fusion.32
  262.4 1.3 fusion.16
  263.9 20.6 %all-gather.2 = bf16[16,1,512]{2,1,0:T(2,128)(2,1)S(1)} all-gather(bf16[1,1,512]{2,1,0:T(2,128)(2,1)S(1)} %reshape.395), channel_id=1, replica_groups=mesh['run'=2,'area'=16] {'area'}, dimensions={0}, use_global_device_ids=true | all-gather | bytes 17408 | tf_op jit(solution)/shard_map/all_gather | solution.py:105
  284.6 1.0 gather_fusion.3
  285.6 4.7 fusion.34
  290.2 1.3 fusion.14
  291.8 17.5 %all-gather.3 = bf16[16,1,512]{2,1,0:T(2,128)(2,1)S(1)} all-gather(bf16[1,1,512]{2,1,0:T(2,128)(2,1)S(1)} %reshape.397), channel_id=1, replica_groups=mesh['run'=2,'area'=16] {'area'}, dimensions={0}, use_global_device_ids=true | all-gather | bytes 17408 | tf_op jit(solution)/shard_map/all_gather | solution.py:105
  309.4 1.0 gather_fusion.4
  310.4 4.7 fusion.36
  315.0 1.3 fusion.12
  316.6 18.9 %all-gather.4 = bf16[16,1,512]{2,1,0:T(2,128)(2,1)S(1)} all-gather(bf16[1,1,512]{2,1,0:T(2,128)(2,1)S(1)} %reshape.399), channel_id=1, replica_groups=mesh['run'=2,'area'=16] {'area'}, dimensions={0}, use_global_device_ids=true | all-gather | bytes 17408 | tf_op jit(solution)/shard_map/all_gather | solution.py:105
  335.5 1.0 gather_fusion.5
  336.5 4.7 fusion.38
  341.2 1.3 fusion.10
  342.7 17.5 %all-gather.5 = bf16[16,1,512]{2,1,0:T(2,128)(2,1)S(1)} all-gather(bf16[1,1,512]{2,1,0:T(2,128)(2,1)S(1)} %reshape.401), channel_id=1, replica_groups=mesh['run'=2,'area'=16] {'area'}, dimensions={0}, use_global_device_ids=true | all-gather | bytes 17408 | tf_op jit(solution)/shard_map/all_gather | solution.py:105
  360.4 1.0 gather_fusion.6
  361.4 4.7 fusion.40
  366.0 1.3 fusion.8
  367.5 19.1 %all-gather.6 = bf16[16,1,512]{2,1,0:T(2,128)(2,1)S(1)} all-gather(bf16[1,1,512]{2,1,0:T(2,128)(2,1)S(1)} %reshape.403), channel_id=1, replica_groups=mesh['run'=2,'area'=16] {'area'}, dimensions={0}, use_global_device_ids=true | all-gather | bytes 17408 | tf_op jit(solution)/shard_map/all_gather | solution.py:105
  386.7 1.0 gather_fusion.7
  387.7 4.7 fusion.42
  392.4 1.3 fusion.6
  393.9 17.5 %all-gather.7 = bf16[16,1,512]{2,1,0:T(2,128)(2,1)S(1)} all-gather(bf16[1,1,512]{2,1,0:T(2,128)(2,1)S(1)} %reshape.405), channel_id=1, replica_groups=mesh['run'=2,'area'=16] {'area'}, dimensions={0}, use_global_device_ids=true | all-gather | bytes 17408 | tf_op jit(solution)/shard_map/all_gather | solution.py:105
  411.5 1.0 gather_fusion.8
  412.5 4.7 fusion.44
  417.2 1.3 fusion.4
  418.7 18.9 %all-gather.8 = bf16[16,1,512]{2,1,0:T(2,128)(2,1)S(1)} all-gather(bf16[1,1,512]{2,1,0:T(2,128)(2,1)S(1)} %reshape.407), channel_id=1, replica_groups=mesh['run'=2,'area'=16] {'area'}, dimensions={0}, use_global_device_ids=true | all-gather | bytes 17408 | tf_op jit(solution)/shard_map/all_gather | solution.py:105
  437.7 1.0 gather_fusion.9
  438.7 4.7 fusion.46
  443.3 1.3 fusion.2
  445.0 17.5 %all-gather.9 = bf16[16,1,512]{2,1,0:T(2,128)(2,1)S(1)} all-gather(bf16[1,1,512]{2,1,0:T(2,128)(2,1)S(1)} %reshape.409), channel_id=1, replica_groups=mesh['run'=2,'area'=16] {'area'}, dimensions={0}, use_global_device_ids=true | all-gather | bytes 17408 | tf_op jit(solution)/shard_map/all_gather | solution.py:105
  462.6 1.0 gather_fusion.10
  463.6 4.7 fusion.48
  468.3 1.3 fusion
  470.9 1.3 stack.43
  (129 shorter events, 5.9 us)
Async XLA Ops:
  34.9 6.7 %copy-start.4 = (s32[10,512]{1,0:T(8,128)S(1)}, s32[10,512]{1,0:T(8,128)}, u32[]{:S(2)}) copy-start(s32[10,512]{1,0:T(8,128)} %param.15) | copy-start | bytes 61444
  34.9 6.8 %copy-start.1 = (f32[512]{0:T(512)S(1)}, f32[512]{0:T(512)}, u32[]{:S(2)}) copy-start(f32[512]{0:T(512)} %param.13) | copy-start | bytes 6148
  34.9 6.8 %copy-start.7 = (f32[512]{0:T(512)S(1)}, f32[512]{0:T(512)}, u32[]{:S(2)}) copy-start(f32[512]{0:T(512)} %param.14) | copy-start | bytes 6148
  34.9 6.8 %copy-start.2 = (s32[2048,1]{0,1:T(1,128)S(1)}, s32[2048,1]{0,1:T(1,128)}, u32[]{:S(2)}) copy-start(s32[2048,1]{0,1:T(1,128)} %param.9) | copy-start | bytes 24580
  34.9 6.8 %copy-start.5 = (s32[2048]{0:T(1024)S(1)}, s32[2048]{0:T(1024)}, u32[]{:S(2)}) copy-start(s32[2048]{0:T(1024)} %param.10) | copy-start | bytes 24580
  34.9 6.8 %copy-start.6 = (s32[2048]{0:T(1024)S(1)}, s32[2048]{0:T(1024)}, u32[]{:S(2)}) copy-start(s32[2048]{0:T(1024)} %param.11) | copy-start | bytes 24580
  34.9 199.5 %copy-start = (s32[8192]{0:T(1024)S(1)}, s32[8192]{0:T(1024)}, u32[]{:S(2)}) copy-start(s32[8192]{0:T(1024)} %param.12) | copy-start | bytes 98308
  34.9 200.5 %all-to-all-start = ((bf16[16,16,128,128]{3,2,1,0:T(8,128)(2,1)}), bf16[16,16,128,128]{3,2,1,0:T(8,128)(2,1)}, u32[]{:S(2)}, u32[]{:S(2)}) async-start(bf16[16,16,128,128]{3,2,1,0:T(8,128)(2,1)} %bitcast.104), calls=%async_computation | async-start | bytes 16777216 | tf_op jit(solution)/shard_map/all_to_all | solution.py:88
  233.5 23.3 %copy-start.3 = (s32[1024]{0:T(1024)}, s32[1024]{0:T(1024)S(1)}, u32[]{:S(2)}) copy-start(s32[1024]{0:T(1024)S(1)} %pad_clamp_fusion) | copy-start | bytes 12292
where the time goes:
time: 478 us; the launch traced here: 472 us
  blocking collectives  353 us (74%)
  matrix products  59.8 us (13%)
  local copies, waits for them, and re-layouts  37.1 us (8%)
  other arithmetic  14.1 us (3%)
  starting transfers between devices  6.68 us (1%)
    all_gather x10, blocking collectives, body(): piece = lax.all_gather(spikes, 'area', axis=0, tiled=True)  353 us
    dot_general x10, matrix products, lag_product(): jnp.einsum('sci,sij->scj', sorted_in, weights, preferred_element_type=jnp...  46.6 us
    scatter x1, local copies, waits for them, and re-layouts, body(): jnp.zeros((slot_count, BLK, BLK), jnp.bfloat16).at[destination].set(weights)  19.3 us
    dot_general x10, matrix products, collect(): jnp.einsum('sb,scj->bcj', target_hot, terms, precision=lax.Precision.HIGH...  13.3 us
    gather x10, local copies, waits for them, and re-layouts, body(): piece_rows[jnp.arange(span, dtype=jnp.int32) // capacity * block_count +...  9.66 us
  transfers between devices with their start and end apart: 1, of which 0 were waited for; matrix products, arithmetic and copies ran while one was open for 1% of the time, Pallas kernels for 0%

commit v1 on v0

v1 whole, which is shorter than its diff:
```python
import functools
import math

import jax
import jax.numpy as jnp
from jax import lax
from jax.experimental import pallas as pl
from jax.experimental.pallas import tpu as pltpu
from jax.sharding import PartitionSpec as P

BLK = 128
NB = 4
DELAYS = 15
ROWS = 16

step_ms = 0.1
ext_gain = 0.25
threshold = 1.0
slope = 4.0
reset_part = 0.5
inhib_gain = 3.0

CHUNKS = 8


def kernel(
    areas,
    edges,
    steps,
    pattern,
    route,
    tgt,
    src,
    lag,
    tau,
    v_init,
    ext,
    volt_out,
    act_out,
    pend_out,
    raw,
    weights,
    hot,
    inputs,
    terms,
    shift,
    q_lag,
    due,
    acts,
    inbox,
    pend_in,
    load_sem,
    send_sem,
    recv_sem,
    fin_send,
    fin_recv,
):
    me = lax.axis_index("area")
    local = NB * BLK
    targets = NB * areas
    per = edges // CHUNKS

    def load(k):
        return pltpu.make_async_copy(
            pattern.at[pl.ds(k * per, per)], raw.at[pl.ds(k * per, per)], load_sem.at[k]
        )

    for k in range(CHUNKS):
        load(k).start()

    barrier = pltpu.get_barrier_semaphore()

    def greet(k, carry):
        peer = lax.rem(me + k, areas)
        pl.semaphore_signal(
            barrier, inc=1, device_id={"area": peer}, device_id_type=pl.DeviceIdType.MESH
        )
        return carry

    lax.fori_loop(1, areas, greet, 0)

    where_to = route[pl.ds(me, 1), :] + areas * tgt[pl.ds(me, 1), :]
    ids = lax.broadcasted_iota(jnp.int32, (targets, edges), 0)
    one_hot = (ids == where_to).astype(jnp.float32).astype(jnp.bfloat16)
    hot[:, :edges] = one_hot
    hot[:, edges:] = one_hot
    for b in range(NB):
        turned = 2 * lag[pl.ds(b, areas, stride=NB), :]
        turned = jnp.where(turned >= DELAYS, turned - DELAYS, turned)
        turned = jnp.where(turned >= DELAYS, turned - DELAYS, turned)
        shift[pl.ds(b * areas, areas), :] = turned
    due[...] = jnp.zeros_like(due)
    own_class = []
    for b in range(NB):
        row = lag[pl.ds(me * NB + b, 1), :]
        own_class.append(jnp.where(row >= DELAYS, row - DELAYS, row))
    classes = lax.broadcasted_iota(jnp.int32, (ROWS, BLK), 0)
    alpha = jnp.exp(-step_ms / tau[...])

    factor = 8.0 / math.sqrt(BLK * edges / NB)
    for k in range(CHUNKS):
        load(k).wait()

        def build(n, carry):
            e = k * per + n
            sign = jnp.where(src[me * edges + e] == NB - 1, -inhib_gain, 1.0)
            mag = jnp.maximum(raw[e].astype(jnp.float32) - 999.0, 0.0)
            weights[e] = (mag * (sign * (factor / 1000.0))).astype(jnp.bfloat16)
            return carry

        lax.fori_loop(0, per, build, 0)

    pl.semaphore_wait(barrier, areas - 1)

    def message(t, peer, slot):
        return pltpu.make_async_remote_copy(
            src_ref=due.at[0, pl.ds(peer, 1), :],
            dst_ref=inbox.at[t, pl.ds(me, 1), :],
            send_sem=send_sem.at[slot],
            recv_sem=recv_sem.at[t, me],
            device_id={"area": peer},
            device_id_type=pl.DeviceIdType.MESH,
        )

    def arrival(t, peer):
        return pltpu.make_async_remote_copy(
            src_ref=due.at[0, pl.ds(me, 1), :],
            dst_ref=inbox.at[t, pl.ds(peer, 1), :],
            send_sem=send_sem.at[0],
            recv_sem=recv_sem.at[t, peer],
            device_id={"area": peer},
            device_id_type=pl.DeviceIdType.MESH,
        )

    def step_to(t, volt, arrived):
        volt = alpha * volt + arrived + ext_gain * (ext[pl.ds(t, 1), :].astype(jnp.float32) - 1.5)
        rate = jax.nn.sigmoid(slope * (volt - threshold))
        volt = volt - reset_part * rate
        acts[pl.ds(t, 1), :] = rate
        for b in range(NB):
            part = rate[:, b * BLK : (b + 1) * BLK]
            inputs[b] = jnp.where(classes == own_class[b], part, 0.0).astype(jnp.bfloat16)

        def multiply(e, carry):
            terms[pl.ds(pl.multiple_of(e * ROWS, ROWS), ROWS), :] = jnp.dot(
                inputs[src[me * edges + e]], weights[e], preferred_element_type=jnp.float32
            )
            return carry

        lax.fori_loop(0, edges, multiply, 0, unroll=8)

        for c in range(DELAYS):
            term = terms[pl.ds(c, edges, stride=ROWS), :]
            high = term.astype(jnp.bfloat16)
            low = (term - high.astype(jnp.float32)).astype(jnp.bfloat16)
            q_lag[c] = jnp.dot(
                hot[...],
                jnp.concatenate([high, low], axis=0),
                preferred_element_type=jnp.float32,
            )

        for b in range(NB):
            lanes = pl.ds(b * BLK, BLK)

            def turn(r, carry):
                rows = pl.ds(pl.multiple_of(b * areas + r * 8, 8), 8)
                by = shift[rows, :]
                q = [q_lag[c, rows, :] for c in range(DELAYS)]
                for bit in range(4):
                    on = (by & (1 << bit)) != 0
                    q = [jnp.where(on, q[(m - (1 << bit)) % DELAYS], q[m]) for m in range(DELAYS)]
                to = pl.ds(pl.multiple_of(r * 8, 8), 8)
                for m in range(DELAYS):
                    old = due[m + 1, to, lanes] if m < DELAYS - 1 else 0.0
                    due[m, to, lanes] = old + q[m]
                return carry

            lax.fori_loop(0, areas // 8, turn, 0)
        return volt

    def one_step(t, volt):
        def send(k, carry):
            message(t, lax.rem(me + k, areas), k).start()
            return carry

        def receive(k, carry):
            arrival(t, lax.rem(me + k, areas)).wait_recv()
            return carry

        def sent(k, carry):
            message(t, lax.rem(me + k, areas), k).wait_send()
            return carry

        lax.fori_loop(1, areas, send, 0)
        inbox[t, pl.ds(me, 1), :] = due[0, pl.ds(me, 1), :]
        lax.fori_loop(1, areas, receive, 0)
        lax.fori_loop(1, areas, sent, 0)
        arrived = jnp.sum(inbox[t], axis=0, keepdims=True)
        return step_to(t + 1, volt, arrived)

    volt = step_to(0, v_init[...], 0.0)
    volt = lax.fori_loop(0, steps - 1, one_step, volt)

    def final(peer, slot):
        return pltpu.make_async_remote_copy(
            src_ref=due.at[:, pl.ds(peer, 1), :],
            dst_ref=pend_in.at[:, pl.ds(me, 1), :],
            send_sem=fin_send.at[slot],
            recv_sem=fin_recv.at[me],
            device_id={"area": peer},
            device_id_type=pl.DeviceIdType.MESH,
        )

    def final_from(peer):
        return pltpu.make_async_remote_copy(
            src_ref=due.at[:, pl.ds(me, 1), :],
            dst_ref=pend_in.at[:, pl.ds(peer, 1), :],
            send_sem=fin_send.at[0],
            recv_sem=fin_recv.at[peer],
            device_id={"area": peer},
            device_id_type=pl.DeviceIdType.MESH,
        )

    def send_final(k, carry):
        final(lax.rem(me + k, areas), k).start()
        return carry

    def receive_final(k, carry):
        final_from(lax.rem(me + k, areas)).wait_recv()
        return carry

    def sent_final(k, carry):
        final(lax.rem(me + k, areas), k).wait_send()
        return carry

    lax.fori_loop(1, areas, send_final, 0)
    volt_out[...] = volt
    act_out[...] = acts[pl.ds(0, steps), :].astype(jnp.bfloat16)
    for m in range(DELAYS):
        pend_in[m, pl.ds(me, 1), :] = due[m, pl.ds(me, 1), :]
    lax.fori_loop(1, areas, receive_final, 0)
    for m in range(DELAYS):
        pend_out[pl.ds(m, 1), :] = jnp.sum(pend_in[m], axis=0, keepdims=True)
    lax.fori_loop(1, areas, sent_final, 0)


def body(pattern, target_area, source_block, target_block, neuron_lag, tau_mem, v_init, ext_count):
    areas = lax.axis_size("area")
    edges = pattern.shape[0]
    steps, local = ext_count.shape
    vmem = pl.BlockSpec(memory_space=pltpu.VMEM)
    targets = areas * NB
    volt, act, pend = pl.pallas_call(
        functools.partial(kernel, areas, edges, steps),
        out_shape=(
            jax.ShapeDtypeStruct((1, local), jnp.float32),
            jax.ShapeDtypeStruct((steps, local), jnp.bfloat16),
            jax.ShapeDtypeStruct((DELAYS, local), jnp.float32),
        ),
        in_specs=[
            pl.BlockSpec(memory_space=pl.ANY),
            vmem,
            vmem,
            pl.BlockSpec(memory_space=pltpu.SMEM),
            vmem,
            vmem,
            vmem,
            vmem,
        ],
        out_specs=(vmem, vmem, vmem),
        scratch_shapes=[
            pltpu.VMEM((edges, BLK, BLK), jnp.int32),
            pltpu.VMEM((edges, BLK, BLK), jnp.bfloat16),
            pltpu.VMEM((targets, 2 * edges), jnp.bfloat16),
            pltpu.VMEM((NB, ROWS, BLK), jnp.bfloat16),
            pltpu.VMEM((edges * ROWS, BLK), jnp.float32),
            pltpu.VMEM((targets, BLK), jnp.int32),
            pltpu.VMEM((DELAYS, targets, BLK), jnp.float32),
            pltpu.VMEM((DELAYS, areas, local), jnp.float32),
            pltpu.VMEM((16, local), jnp.float32),
            pltpu.VMEM((steps - 1, areas, local), jnp.float32),
            pltpu.VMEM((DELAYS, areas, local), jnp.float32),
            pltpu.SemaphoreType.DMA((CHUNKS,)),
            pltpu.SemaphoreType.DMA((areas,)),
            pltpu.SemaphoreType.DMA((steps - 1, areas)),
            pltpu.SemaphoreType.DMA((areas,)),
            pltpu.SemaphoreType.DMA((areas,)),
        ],
        compiler_params=pltpu.CompilerParams(
            collective_id=0, has_side_effects=True, vmem_limit_bytes=48 * 1024 * 1024
        ),
    )(
        pattern,
        target_area.reshape(areas, edges),
        target_block.reshape(areas, edges),
        source_block,
        neuron_lag.reshape(targets, BLK),
        tau_mem.reshape(1, local),
        v_init.reshape(1, local),
        ext_count,
    )
    return (volt.reshape(local), act, pend)


def solution(mesh):
    in_specs = (
        P("area", None, None),
        P(),
        P(),
        P(),
        P(),
        P("area"),
        P(("run", "area")),
        P(None, ("run", "area")),
    )
    out_specs = (P(("run", "area")), P(None, ("run", "area")), P(None, ("run", "area")))
    return jax.shard_map(body, mesh=mesh, in_specs=in_specs, out_specs=out_specs, check_vma=False)
```

time: 478 us -> 101 us (0.21); the launches traced: 472 us -> 101 us
  blocking collectives: 353 us -> 0 us
  Pallas kernels: 0 us -> 93.6 us
  matrix products: 59.8 us -> 0 us
  local copies, waits for them, and re-layouts: 37.1 us -> 6.76 us
  other arithmetic: 14.1 us -> 0 us
  starting transfers between devices: 6.68 us -> 0 us
    all_gather x10 -> x0, blocking collectives: 353 us -> none  [body(): piece = lax.all_gather(spikes, 'area', axis=0, tiled=True)]
    pallas_call x0 -> x1, Pallas kernels: none -> 93.6 us  [body(): pl.pallas_call(functools.partial(kernel, areas, edges, steps), out_shape=...]
    dot_general x20 -> x0, matrix products: 59.8 us -> none  [the longest x10 46.6 us: lag_product(): jnp.einsum('sci,sij->scj', sorted_in, weights, preferred_element_type=jnp...]
    scatter x1 -> x0, local copies, waits for them, and re-layouts: 19.3 us -> none  [body(): jnp.zeros((slot_count, BLK, BLK), jnp.bfloat16).at[destination].set(weights)]
    gather x11 -> x0, local copies, waits for them, and re-layouts: 10.4 us -> none  [the longest x10 9.66 us: body(): piece_rows[jnp.arange(span, dtype=jnp.int32) // capacity * block_count +...]
    convert_element_type x11 -> x0, other arithmetic: 6.98 us -> none  [the longest x1 6.73 us: block_weights(): return (factor * magnitude * signs[:, None, None]).astype(jnp.bfloat16)]
    all_to_all x1 -> x0, starting transfers between devices: 6.68 us -> none  [body(): lax.all_to_all(outbox.reshape(area_count, capacity, BLK, BLK), 'area', sp...]
    unnamed x36 -> x17, local copies, waits for them, and re-layouts: 0.17 us -> 6.76 us
  transfers between devices with their start and end apart: 1 -> 0, of which waited for: 0 -> 0; matrix products, arithmetic and copies ran while one was open for 1% -> 0% of each run, Pallas kernels for 0% -> 0%
where the time goes in v1:
time: 101 us
  Pallas kernels  93.6 us (93%)
  local copies, waits for them, and re-layouts  6.76 us (7%)
    pallas_call x1, Pallas kernels, body(): pl.pallas_call(functools.partial(kernel, areas, edges, steps), out_shape=...  93.6 us
    unnamed x17, local copies, waits for them, and re-layouts  6.76 us

profile of v1, /device:TPU:11, one launch (start us, length us, event | category | flops | bytes accessed | tf_op | source)
XLA Modules:
  0.0 101.0 jit_solution(3425463155136623833)
XLA Ops:
  0.6 0.0 copy-start
  0.6 0.7 copy-done
  1.4 0.0 copy-start.1
  1.4 0.8 copy-done.1
  2.2 0.0 copy-start.2
  2.2 0.7 copy-done.2
  2.8 0.0 copy-start.3
  2.9 0.7 copy-done.3
  3.5 0.0 copy-start.4
  3.5 0.7 copy-done.4
  4.2 0.0 copy-start.5
  4.2 0.7 copy-done.5
  4.9 0.0 copy-start.6
  4.9 0.7 copy-done.6
  5.6 93.6 %shard_map.103 = (f32[1,512]{1,0:T(1,128)S(1)}, bf16[10,512]{1,0:T(8,128)(2,1)S(1)}, f32[15,512]{1,0:T(8,128)S(1)}) custom-call(s32[128,128,128]{2,1,0:T(8,128)} %pattern.1, s32[16,128]{1,0:T(8,128)S(1)} %bitcast.7, s32[16,128]{1,0:T(8,128)S(1)} %bitcast.8, s32[2048]{0:T(1024)S(1)} %copy-done.4, s32[64,128]{1,0:T(8,128)S(1)} %bitcast.6, ...), custom_call_target="tpu_custom_call" | custom-call | tf_op jit(solution)/shard_map/pallas_call | solution.py:253
  99.2 0.6 copy.14
  99.8 0.6 copy.15
  100.4 0.6 copy.16
Async XLA Ops:
  0.6 0.8 copy-start
  1.4 0.8 copy-start.1
  2.2 0.7 copy-start.2
  2.8 0.7 copy-start.3
  3.5 0.7 copy-start.4
  4.2 0.7 copy-start.5
  4.9 0.7 copy-start.6

commit v2 on v1

v2 whole, which is shorter than its diff:
```python
import functools
import math

import jax
import jax.numpy as jnp
from jax import lax
from jax.experimental import pallas as pl
from jax.experimental.pallas import tpu as pltpu
from jax.sharding import PartitionSpec as P

BLK = 128
NB = 4
DELAYS = 15
ROWS = 16

step_ms = 0.1
ext_gain = 0.25
threshold = 1.0
slope = 4.0
reset_part = 0.5
inhib_gain = 3.0

CHUNKS = 8


def side_by_side(x):
    return jnp.concatenate([x[b : b + 1, :] for b in range(NB)], axis=1)


def stacked(x):
    return jnp.concatenate([x[:, b * BLK : (b + 1) * BLK] for b in range(NB)], axis=0)


def split(x):
    high = x.astype(jnp.bfloat16)
    low = (x - high.astype(jnp.float32)).astype(jnp.bfloat16)
    return jnp.concatenate([high, low], axis=0)


def kernel(
    areas,
    edges,
    steps,
    pattern,
    route_in,
    tgt_in,
    src_in,
    lag_in,
    tau_in,
    v_in,
    ext_in,
    volt_out,
    act_out,
    pend_out,
    raw,
    weights,
    route,
    tgt,
    src,
    lag,
    tau,
    v_init,
    ext,
    hot,
    inputs,
    terms,
    shift,
    first,
    drive,
    q_lag,
    due,
    acts,
    outbox,
    inbox,
    pend_go,
    pend_in,
    small_sem,
    load_sem,
    send_sem,
    recv_sem,
    fin_send,
    fin_recv,
):
    me = lax.axis_index("area")
    targets = NB * areas
    per = edges // CHUNKS

    small = [
        pltpu.make_async_copy(a, b, small_sem.at[k])
        for k, (a, b) in enumerate(
            [
                (src_in, src),
                (lag_in, lag),
                (route_in, route),
                (tgt_in, tgt),
                (tau_in, tau),
                (v_in, v_init),
                (ext_in, ext),
            ]
        )
    ]
    for copy in small:
        copy.start()

    def load(k):
        return pltpu.make_async_copy(
            pattern.at[pl.ds(k * per, per)], raw.at[pl.ds(k * per, per)], load_sem.at[k]
        )

    for k in range(CHUNKS):
        load(k).start()

    def peer_at(k):
        p = me + k
        return jnp.where(p >= areas, p - areas, p)

    def every_peer(act):
        if areas <= 16:
            for k in sorted(range(1, areas), key=lambda k: abs(2 * k - areas)):
                act(peer_at(k))
        else:

            def one(k, carry):
                act(peer_at(k))
                return carry

            lax.fori_loop(1, areas, one, 0)

    barrier = pltpu.get_barrier_semaphore()

    def greet(peer):
        pl.semaphore_signal(
            barrier, inc=1, device_id={"area": peer}, device_id_type=pl.DeviceIdType.MESH
        )

    every_peer(greet)
    for copy in small:
        copy.wait()

    where_to = NB * route[pl.ds(me, 1), :] + tgt[pl.ds(me, 1), :]
    ids = lax.broadcasted_iota(jnp.int32, (targets, edges), 0)
    one_hot = (ids == where_to).astype(jnp.float32).astype(jnp.bfloat16)
    hot[:, :edges] = one_hot
    hot[:, edges:] = one_hot
    turned = 2 * lag[...]
    turned = jnp.where(turned >= DELAYS, turned - DELAYS, turned)
    turned = jnp.where(turned >= DELAYS, turned - DELAYS, turned)
    shift[...] = turned
    at_once = jnp.where(turned == 0, 0, DELAYS - turned)
    first[...] = lax.dot_general(
        one_hot,
        at_once.astype(jnp.float32).astype(jnp.bfloat16),
        (((0,), (0,)), ((), ())),
        preferred_element_type=jnp.float32,
    )
    due[...] = jnp.zeros_like(due)
    own_class = []
    for b in range(NB):
        row = lag[pl.ds(me * NB + b, 1), :]
        own_class.append(jnp.where(row >= DELAYS, row - DELAYS, row))
    classes = lax.broadcasted_iota(jnp.int32, (ROWS, BLK), 0)
    alpha = jnp.exp(-step_ms / stacked(tau[...]))
    for t in range(steps):
        drive[t] = ext_gain * (stacked(ext[pl.ds(t, 1), :]).astype(jnp.float32) - 1.5)

    factor = 8.0 / math.sqrt(BLK * edges / NB)
    for k in range(CHUNKS):
        load(k).wait()

        def build(n, carry):
            g = k * (per // 2) + n
            for half in range(2):
                e = 2 * g + half
                sign = jnp.where(src[me * edges + e] == NB - 1, -inhib_gain, 1.0)
                mag = jnp.maximum(raw[e].astype(jnp.float32) - 999.0, 0.0)
                weights[g, pl.ds(half * BLK, BLK), :] = (mag * (sign * (factor / 1000.0))).astype(
                    jnp.bfloat16
                )
            return carry

        lax.fori_loop(0, per // 2, build, 0)

    def think(t, volt, arrived):
        volt = alpha * volt + arrived + drive[t]
        rate = jax.nn.sigmoid(slope * (volt - threshold))
        volt = volt - reset_part * rate
        for b in range(NB):
            inputs[b] = jnp.where(classes == own_class[b], rate[b : b + 1, :], 0.0).astype(
                jnp.bfloat16
            )
        none = jnp.zeros((ROWS, BLK), jnp.bfloat16)

        def multiply(g, carry):
            upper = inputs[src[me * edges + 2 * g]]
            lower = inputs[src[me * edges + 2 * g + 1]]
            both = jnp.concatenate(
                [
                    jnp.concatenate([upper, none], axis=1),
                    jnp.concatenate([none, lower], axis=1),
                ],
                axis=0,
            )
            rows = pl.ds(pl.multiple_of(g * (2 * ROWS), 2 * ROWS), 2 * ROWS)
            terms[rows, :] = jnp.dot(both, weights[g], preferred_element_type=jnp.float32)
            return carry

        lax.fori_loop(0, edges // 2, multiply, 0, unroll=32)
        return volt, rate

    def gather_lags():
        for c in range(DELAYS):
            q_lag[c] = jnp.dot(
                hot[...],
                split(terms[pl.ds(c, edges, stride=ROWS), :]),
                preferred_element_type=jnp.float32,
            )

    def arrivals(rows):
        by = shift[rows, :]
        q = [q_lag[c, rows, :] for c in range(DELAYS)]
        for bit in range(4):
            on = (by & (1 << bit)) != 0
            q = [jnp.where(on, q[(m - (1 << bit)) % DELAYS], q[m]) for m in range(DELAYS)]
        for m in range(DELAYS - 1):
            q[m] = q[m] + due[m + 1, rows, :]
        return q

    def one_step(t, carry):
        volt, arrived = carry
        volt, rate = think(t, volt, arrived)
        picked = []
        for e in range(0, edges, 32):
            mine = first[pl.ds(e, 32), :]
            y = jnp.zeros((32, BLK), jnp.float32)
            for c in range(DELAYS):
                y = jnp.where(mine == float(c), terms[pl.ds(e * ROWS + c, 32, stride=ROWS), :], y)
            picked.append(y)
        soon = due[1] + jnp.dot(
            hot[...], split(jnp.concatenate(picked, axis=0)), preferred_element_type=jnp.float32
        )
        for a in range(areas):
            outbox[t, a] = soon[a * NB : (a + 1) * NB, :]

        def send(peer):
            pltpu.make_async_remote_copy(
                src_ref=outbox.at[t, peer],
                dst_ref=inbox.at[t, me],
                send_sem=send_sem.at[t],
                recv_sem=recv_sem.at[t],
                device_id={"area": peer},
                device_id_type=pl.DeviceIdType.MESH,
            ).start()

        every_peer(send)
        inbox[t, me] = outbox[t, me]
        acts[pl.ds(t, 1), :] = side_by_side(rate)
        gather_lags()

        def turn(r, carry):
            rows = pl.ds(pl.multiple_of(r * 8, 8), 8)
            q = arrivals(rows)
            for m in range(DELAYS):
                due[m, rows, :] = q[m]
            return carry

        lax.fori_loop(0, targets // 8, turn, 0)
        step_messages(t).wait_recv()
        return volt, jnp.sum(inbox[t], axis=0)

    def step_messages(t):
        return pltpu.make_async_remote_copy(
            src_ref=outbox.at[t, pl.ds(0, areas - 1)],
            dst_ref=inbox.at[t, pl.ds(0, areas - 1)],
            send_sem=send_sem.at[t],
            recv_sem=recv_sem.at[t],
            device_id={"area": me},
            device_id_type=pl.DeviceIdType.MESH,
        )

    pl.semaphore_wait(barrier, areas - 1)
    volt, arrived = lax.fori_loop(
        0, steps - 1, one_step, (stacked(v_init[...]), jnp.zeros((NB, BLK), jnp.float32))
    )
    volt, rate = think(steps - 1, volt, arrived)
    gather_lags()

    def last(n, carry):
        r = n + me // 2 + 1
        r = jnp.where(r >= areas // 2, r - areas // 2, r)
        q = arrivals(pl.ds(pl.multiple_of(r * 8, 8), 8))
        for half in range(2):
            peer = 2 * r + half
            for m in range(DELAYS):
                pend_go[peer, m] = q[m][half * NB : (half + 1) * NB, :]

            @pl.when(peer != me)
            def _():
                pltpu.make_async_remote_copy(
                    src_ref=pend_go.at[peer],
                    dst_ref=pend_in.at[me],
                    send_sem=fin_send,
                    recv_sem=fin_recv,
                    device_id={"area": peer},
                    device_id_type=pl.DeviceIdType.MESH,
                ).start()

        return carry

    lax.fori_loop(0, areas // 2, last, 0)
    acts[pl.ds(steps - 1, 1), :] = side_by_side(rate)
    pend_in[me] = pend_go[me]
    volt_out[...] = side_by_side(volt)
    act_out[...] = acts[pl.ds(0, steps), :].astype(jnp.bfloat16)
    for t in range(steps - 1):
        step_messages(t).wait_send()
    everything = pltpu.make_async_remote_copy(
        src_ref=pend_go.at[pl.ds(0, areas - 1)],
        dst_ref=pend_in.at[pl.ds(0, areas - 1)],
        send_sem=fin_send,
        recv_sem=fin_recv,
        device_id={"area": me},
        device_id_type=pl.DeviceIdType.MESH,
    )
    everything.wait_recv()
    for m in range(DELAYS):
        pend_out[pl.ds(m, 1), :] = side_by_side(jnp.sum(pend_in[:, m], axis=0))
    everything.wait_send()


def body(pattern, target_area, source_block, target_block, neuron_lag, tau_mem, v_init, ext_count):
    areas = lax.axis_size("area")
    edges = pattern.shape[0]
    steps, local = ext_count.shape
    vmem = pl.BlockSpec(memory_space=pltpu.VMEM)
    hbm = pl.BlockSpec(memory_space=pltpu.HBM)
    targets = areas * NB
    f32 = jnp.float32
    volt, act, pend = pl.pallas_call(
        functools.partial(kernel, areas, edges, steps),
        out_shape=(
            jax.ShapeDtypeStruct((1, local), f32),
            jax.ShapeDtypeStruct((steps, local), jnp.bfloat16),
            jax.ShapeDtypeStruct((DELAYS, local), f32),
        ),
        in_specs=[hbm] * 8,
        out_specs=(vmem, vmem, vmem),
        scratch_shapes=[
            pltpu.VMEM((edges, BLK, BLK), jnp.int32),
            pltpu.VMEM((edges // 2, 2 * BLK, BLK), jnp.bfloat16),
            pltpu.VMEM((areas, edges), jnp.int32),
            pltpu.VMEM((areas, edges), jnp.int32),
            pltpu.SMEM((areas * edges,), jnp.int32),
            pltpu.VMEM((targets, BLK), jnp.int32),
            pltpu.VMEM((1, local), f32),
            pltpu.VMEM((1, local), f32),
            pltpu.VMEM((steps, local), jnp.int32),
            pltpu.VMEM((targets, 2 * edges), jnp.bfloat16),
            pltpu.VMEM((NB, ROWS, BLK), jnp.bfloat16),
            pltpu.VMEM((edges * ROWS, BLK), f32),
            pltpu.VMEM((targets, BLK), jnp.int32),
            pltpu.VMEM((edges, BLK), f32),
            pltpu.VMEM((steps, NB, BLK), f32),
            pltpu.VMEM((DELAYS, targets, BLK), f32),
            pltpu.VMEM((DELAYS, targets, BLK), f32),
            pltpu.VMEM((16, local), f32),
            pltpu.VMEM((steps - 1, areas, NB, BLK), f32),
            pltpu.VMEM((steps - 1, areas, NB, BLK), f32),
            pltpu.VMEM((areas, DELAYS, NB, BLK), f32),
            pltpu.VMEM((areas, DELAYS, NB, BLK), f32),
            pltpu.SemaphoreType.DMA((7,)),
            pltpu.SemaphoreType.DMA((CHUNKS,)),
            pltpu.SemaphoreType.DMA((steps - 1,)),
            pltpu.SemaphoreType.DMA((steps - 1,)),
            pltpu.SemaphoreType.DMA,
            pltpu.SemaphoreType.DMA,
        ],
        compiler_params=pltpu.CompilerParams(
            collective_id=0, has_side_effects=True, vmem_limit_bytes=48 * 1024 * 1024
        ),
    )(
        pattern,
        target_area.reshape(areas, edges),
        target_block.reshape(areas, edges),
        source_block,
        neuron_lag.reshape(targets, BLK),
        tau_mem.reshape(1, local),
        v_init.reshape(1, local),
        ext_count,
    )
    return (volt.reshape(local), act, pend)


def solution(mesh):
    in_specs = (
        P("area", None, None),
        P(),
        P(),
        P(),
        P(),
        P("area"),
        P(("run", "area")),
        P(None, ("run", "area")),
    )
    out_specs = (P(("run", "area")), P(None, ("run", "area")), P(None, ("run", "area")))
    return jax.shard_map(body, mesh=mesh, in_specs=in_specs, out_specs=out_specs, check_vma=False)
```

time: 101 us -> 75.4 us (0.75)
  Pallas kernels: 93.6 us -> 67.5 us
    pallas_call x1, Pallas kernels: 93.6 us -> 67.5 us  [body(): pl.pallas_call(functools.partial(kernel, areas, edges, steps), out_shape=...]
where the time goes in v2:
time: 75.4 us; the launch traced here: 75 us
  Pallas kernels  67.5 us (90%)
  local copies, waits for them, and re-layouts  6.76 us (9%)
    pallas_call x1, Pallas kernels, body(): pl.pallas_call(functools.partial(kernel, areas, edges, steps), out_shape=...  67.5 us
    unnamed x17, local copies, waits for them, and re-layouts  6.76 us

profile of v2, /device:TPU:11, one launch (start us, length us, event | category | flops | bytes accessed | tf_op | source)
XLA Modules:
  0.0 75.0 jit_solution(10468395329144245223)
XLA Ops:
  0.6 0.0 copy-start
  0.6 0.7 copy-done
  1.4 0.0 copy-start.1
  1.4 0.8 %copy-done.1 = s32[10,512]{1,0:T(8,128)S(1)} copy-done((s32[10,512]{1,0:T(8,128)S(1)}, s32[10,512]{1,0:T(8,128)}, u32[]{:S(2)}) %copy-start.1) | copy-done | bytes 20504
  2.2 0.0 copy-start.2
  2.2 0.7 copy-done.2
  2.8 0.0 copy-start.3
  2.9 0.7 copy-done.3
  3.5 0.0 copy-start.4
  3.5 0.7 copy-done.4
  4.2 0.0 copy-start.5
  4.2 0.7 copy-done.5
  4.9 0.0 copy-start.6
  4.9 0.7 copy-done.6
  5.6 67.5 %shard_map.103 = (f32[1,512]{1,0:T(1,128)S(1)}, bf16[10,512]{1,0:T(8,128)(2,1)S(1)}, f32[15,512]{1,0:T(8,128)S(1)}) custom-call(s32[128,128,128]{2,1,0:T(8,128)} %pattern.1, s32[16,128]{1,0:T(8,128)S(1)} %bitcast.7, s32[16,128]{1,0:T(8,128)S(1)} %bitcast.8, s32[2048]{0:T(1024)S(1)} %copy-done.4, s32[64,128]{1,0:T(8,128)S(1)} %bitcast.6, ...), custom_call_target="tpu_custom_call" | custom-call | tf_op jit(solution)/shard_map/pallas_call | solution.py:338
  73.2 0.6 copy.14
  73.7 0.6 copy.15
  74.3 0.6 copy.16
Async XLA Ops:
  0.6 0.8 %copy-start = (s32[8192]{0:T(1024)S(1)}, s32[8192]{0:T(1024)}, u32[]{:S(2)}) copy-start(s32[8192]{0:T(1024)} %param.12) | copy-start | bytes 98308
  1.4 0.8 %copy-start.1 = (s32[10,512]{1,0:T(8,128)S(1)}, s32[10,512]{1,0:T(8,128)}, u32[]{:S(2)}) copy-start(s32[10,512]{1,0:T(8,128)} %ext_in.1) | copy-start | bytes 61444
  2.2 0.7 copy-start.2
  2.8 0.7 copy-start.3
  3.5 0.7 copy-start.4
  4.2 0.7 copy-start.5
  4.9 0.7 copy-start.6

commit v3 on v2

--- a/solution.py
+++ b/solution.py
@@ -21,6 +21,7 @@
 inhib_gain = 3.0
 
 CHUNKS = 8
+SHARE = ROWS * NB
 
 
 def side_by_side(x):
@@ -204,7 +205,7 @@
             terms[rows, :] = jnp.dot(both, weights[g], preferred_element_type=jnp.float32)
             return carry
 
-        lax.fori_loop(0, edges // 2, multiply, 0, unroll=32)
+        lax.fori_loop(0, edges // 2, multiply, 0, unroll=64 if areas <= 16 else 32)
         return volt, rate
 
     def gather_lags():
@@ -284,20 +285,24 @@
     volt, rate = think(steps - 1, volt, arrived)
     gather_lags()
 
+    def share(a):
+        return pl.ds(pl.multiple_of(a * SHARE, SHARE), SHARE)
+
     def last(n, carry):
         r = n + me // 2 + 1
         r = jnp.where(r >= areas // 2, r - areas // 2, r)
         q = arrivals(pl.ds(pl.multiple_of(r * 8, 8), 8))
         for half in range(2):
             peer = 2 * r + half
-            for m in range(DELAYS):
-                pend_go[peer, m] = q[m][half * NB : (half + 1) * NB, :]
+            parts = [q[m][half * NB : (half + 1) * NB, :] for m in range(DELAYS)]
+            parts.append(jnp.zeros((NB, BLK), jnp.float32))
+            pend_go[share(peer), :] = jnp.concatenate(parts, axis=0).astype(jnp.bfloat16)
 
             @pl.when(peer != me)
             def _():
                 pltpu.make_async_remote_copy(
-                    src_ref=pend_go.at[peer],
-                    dst_ref=pend_in.at[me],
+                    src_ref=pend_go.at[share(peer)],
+                    dst_ref=pend_in.at[share(me)],
                     send_sem=fin_send,
                     recv_sem=fin_recv,
                     device_id={"area": peer},
@@ -308,22 +313,25 @@
 
     lax.fori_loop(0, areas // 2, last, 0)
     acts[pl.ds(steps - 1, 1), :] = side_by_side(rate)
-    pend_in[me] = pend_go[me]
+    pend_in[share(me), :] = pend_go[share(me), :]
     volt_out[...] = side_by_side(volt)
     act_out[...] = acts[pl.ds(0, steps), :].astype(jnp.bfloat16)
     for t in range(steps - 1):
         step_messages(t).wait_send()
     everything = pltpu.make_async_remote_copy(
-        src_ref=pend_go.at[pl.ds(0, areas - 1)],
-        dst_ref=pend_in.at[pl.ds(0, areas - 1)],
+        src_ref=pend_go.at[pl.ds(0, (areas - 1) * SHARE)],
+        dst_ref=pend_in.at[pl.ds(0, (areas - 1) * SHARE)],
         send_sem=fin_send,
         recv_sem=fin_recv,
         device_id={"area": me},
         device_id_type=pl.DeviceIdType.MESH,
     )
     everything.wait_recv()
+    total = jnp.zeros((SHARE, BLK), jnp.float32)
+    for a in range(areas):
+        total = total + pend_in[pl.ds(a * SHARE, SHARE), :].astype(jnp.float32)
     for m in range(DELAYS):
-        pend_out[pl.ds(m, 1), :] = side_by_side(jnp.sum(pend_in[:, m], axis=0))
+        pend_out[pl.ds(m, 1), :] = side_by_side(total[m * NB : (m + 1) * NB, :])
     everything.wait_send()
 
 
@@ -365,8 +373,8 @@
             pltpu.VMEM((16, local), f32),
             pltpu.VMEM((steps - 1, areas, NB, BLK), f32),
             pltpu.VMEM((steps - 1, areas, NB, BLK), f32),
-            pltpu.VMEM((areas, DELAYS, NB, BLK), f32),
-            pltpu.VMEM((areas, DELAYS, NB, BLK), f32),
+            pltpu.VMEM((areas * SHARE, BLK), jnp.bfloat16),
+            pltpu.VMEM((areas * SHARE, BLK), jnp.bfloat16),
             pltpu.SemaphoreType.DMA((7,)),
             pltpu.SemaphoreType.DMA((CHUNKS,)),
             pltpu.SemaphoreType.DMA((steps - 1,)),

time: 75.4 us -> 68.7 us (0.911)
  Pallas kernels: 67.5 us -> 60.4 us
    pallas_call x1, Pallas kernels: 67.5 us -> 60.4 us  [body(): pl.pallas_call(functools.partial(kernel, areas, edges, steps), out_shape=...]
where the time goes in v3:
time: 68.7 us; the launch traced here: 67.9 us
  Pallas kernels  60.4 us (88%)
  local copies, waits for them, and re-layouts  6.76 us (10%)
    pallas_call x1, Pallas kernels, body(): pl.pallas_call(functools.partial(kernel, areas, edges, steps), out_shape=...  60.4 us
    unnamed x17, local copies, waits for them, and re-layouts  6.76 us

profile of v3, /device:TPU:11, one launch (start us, length us, event | category | flops | bytes accessed | tf_op | source)
XLA Modules:
  0.0 67.9 jit_solution(2360294282364302536)
XLA Ops:
  0.6 0.0 copy-start
  0.6 0.7 %copy-done = s32[8192]{0:T(1024)S(1)} copy-done((s32[8192]{0:T(1024)S(1)}, s32[8192]{0:T(1024)}, u32[]{:S(2)}) %copy-start) | copy-done | bytes 32792
  1.4 0.0 copy-start.1
  1.4 0.8 %copy-done.1 = s32[10,512]{1,0:T(8,128)S(1)} copy-done((s32[10,512]{1,0:T(8,128)S(1)}, s32[10,512]{1,0:T(8,128)}, u32[]{:S(2)}) %copy-start.1) | copy-done | bytes 20504
  2.2 0.0 copy-start.2
  2.2 0.7 %copy-done.2 = s32[2048,1]{0,1:T(1,128)S(1)} copy-done((s32[2048,1]{0,1:T(1,128)S(1)}, s32[2048,1]{0,1:T(1,128)}, u32[]{:S(2)}) %copy-start.2) | copy-done | bytes 8216
  2.8 0.0 copy-start.3
  2.9 0.7 %copy-done.3 = s32[2048]{0:T(1024)S(1)} copy-done((s32[2048]{0:T(1024)S(1)}, s32[2048]{0:T(1024)}, u32[]{:S(2)}) %copy-start.3) | copy-done | bytes 8216
  3.5 0.0 copy-start.4
  3.5 0.7 %copy-done.4 = s32[2048]{0:T(1024)S(1)} copy-done((s32[2048]{0:T(1024)S(1)}, s32[2048]{0:T(1024)}, u32[]{:S(2)}) %copy-start.4) | copy-done | bytes 8216
  4.2 0.0 copy-start.5
  4.2 0.7 %copy-done.5 = f32[512]{0:T(512)S(1)} copy-done((f32[512]{0:T(512)S(1)}, f32[512]{0:T(512)}, u32[]{:S(2)}) %copy-start.5) | copy-done | bytes 2072
  4.9 0.0 copy-start.6
  4.9 0.7 %copy-done.6 = f32[512]{0:T(512)S(1)} copy-done((f32[512]{0:T(512)S(1)}, f32[512]{0:T(512)}, u32[]{:S(2)}) %copy-start.6) | copy-done | bytes 2072
  5.6 60.4 %shard_map.103 = (f32[1,512]{1,0:T(1,128)S(1)}, bf16[10,512]{1,0:T(8,128)(2,1)S(1)}, f32[15,512]{1,0:T(8,128)S(1)}) custom-call(s32[128,128,128]{2,1,0:T(8,128)} %pattern.1, s32[16,128]{1,0:T(8,128)S(1)} %bitcast.7, s32[16,128]{1,0:T(8,128)S(1)} %bitcast.8, s32[2048]{0:T(1024)S(1)} %copy-done.4, s32[64,128]{1,0:T(8,128)S(1)} %bitcast.6, ...), custom_call_target="tpu_custom_call" | custom-call | tf_op jit(solution)/shard_map/pallas_call | solution.py:346
  66.1 0.6 copy.14
  66.6 0.6 copy.15
  67.2 0.6 copy.16
Async XLA Ops:
  0.6 0.8 %copy-start = (s32[8192]{0:T(1024)S(1)}, s32[8192]{0:T(1024)}, u32[]{:S(2)}) copy-start(s32[8192]{0:T(1024)} %param.12) | copy-start | bytes 98308
  1.4 0.8 %copy-start.1 = (s32[10,512]{1,0:T(8,128)S(1)}, s32[10,512]{1,0:T(8,128)}, u32[]{:S(2)}) copy-start(s32[10,512]{1,0:T(8,128)} %ext_in.1) | copy-start | bytes 61444
  2.2 0.7 %copy-start.2 = (s32[2048,1]{0,1:T(1,128)S(1)}, s32[2048,1]{0,1:T(1,128)}, u32[]{:S(2)}) copy-start(s32[2048,1]{0,1:T(1,128)} %param.9) | copy-start | bytes 24580
  2.8 0.7 %copy-start.3 = (s32[2048]{0:T(1024)S(1)}, s32[2048]{0:T(1024)}, u32[]{:S(2)}) copy-start(s32[2048]{0:T(1024)} %param.11) | copy-start | bytes 24580
  3.5 0.7 %copy-start.4 = (s32[2048]{0:T(1024)S(1)}, s32[2048]{0:T(1024)}, u32[]{:S(2)}) copy-start(s32[2048]{0:T(1024)} %src_in.1) | copy-start | bytes 24580
  4.2 0.7 %copy-start.5 = (f32[512]{0:T(512)S(1)}, f32[512]{0:T(512)}, u32[]{:S(2)}) copy-start(f32[512]{0:T(512)} %param.13) | copy-start | bytes 6148
  4.9 0.7 %copy-start.6 = (f32[512]{0:T(512)S(1)}, f32[512]{0:T(512)}, u32[]{:S(2)}) copy-start(f32[512]{0:T(512)} %param.14) | copy-start | bytes 6148

commit v4 on v3

--- a/solution.py
+++ b/solution.py
@@ -117,7 +117,7 @@
 
     def every_peer(act):
         if areas <= 16:
-            for k in sorted(range(1, areas), key=lambda k: abs(2 * k - areas)):
+            for k in sorted(range(1, areas), key=lambda k: -abs(2 * k - areas)):
                 act(peer_at(k))
         else:
 

time: 68.7 us -> 67.7 us (0.985)
  Pallas kernels: 60.4 us -> 59.4 us
    pallas_call x1, Pallas kernels: 60.4 us -> 59.4 us  [body(): pl.pallas_call(functools.partial(kernel, areas, edges, steps), out_shape=...]
where the time goes in v4:
time: 67.7 us; the launch traced here: 66.8 us
  Pallas kernels  59.4 us (88%)
  local copies, waits for them, and re-layouts  6.76 us (10%)
    pallas_call x1, Pallas kernels, body(): pl.pallas_call(functools.partial(kernel, areas, edges, steps), out_shape=...  59.4 us
    unnamed x17, local copies, waits for them, and re-layouts  6.76 us

profile of v4, /device:TPU:11, one launch (start us, length us, event | category | flops | bytes accessed | tf_op | source)
XLA Modules:
  0.0 66.8 jit_solution(9314411481996675375)
XLA Ops:
  0.6 0.0 copy-start
  0.6 0.7 %copy-done = s32[8192]{0:T(1024)S(1)} copy-done((s32[8192]{0:T(1024)S(1)}, s32[8192]{0:T(1024)}, u32[]{:S(2)}) %copy-start) | copy-done | bytes 32792
  1.4 0.0 copy-start.1
  1.4 0.8 %copy-done.1 = s32[10,512]{1,0:T(8,128)S(1)} copy-done((s32[10,512]{1,0:T(8,128)S(1)}, s32[10,512]{1,0:T(8,128)}, u32[]{:S(2)}) %copy-start.1) | copy-done | bytes 20504
  2.2 0.0 copy-start.2
  2.2 0.7 %copy-done.2 = s32[2048,1]{0,1:T(1,128)S(1)} copy-done((s32[2048,1]{0,1:T(1,128)S(1)}, s32[2048,1]{0,1:T(1,128)}, u32[]{:S(2)}) %copy-start.2) | copy-done | bytes 8216
  2.8 0.0 copy-start.3
  2.9 0.7 %copy-done.3 = s32[2048]{0:T(1024)S(1)} copy-done((s32[2048]{0:T(1024)S(1)}, s32[2048]{0:T(1024)}, u32[]{:S(2)}) %copy-start.3) | copy-done | bytes 8216
  3.5 0.0 copy-start.4
  3.5 0.7 %copy-done.4 = s32[2048]{0:T(1024)S(1)} copy-done((s32[2048]{0:T(1024)S(1)}, s32[2048]{0:T(1024)}, u32[]{:S(2)}) %copy-start.4) | copy-done | bytes 8216
  4.2 0.0 copy-start.5
  4.2 0.7 %copy-done.5 = f32[512]{0:T(512)S(1)} copy-done((f32[512]{0:T(512)S(1)}, f32[512]{0:T(512)}, u32[]{:S(2)}) %copy-start.5) | copy-done | bytes 2072
  4.9 0.0 copy-start.6
  4.9 0.7 %copy-done.6 = f32[512]{0:T(512)S(1)} copy-done((f32[512]{0:T(512)S(1)}, f32[512]{0:T(512)}, u32[]{:S(2)}) %copy-start.6) | copy-done | bytes 2072
  5.6 59.4 %shard_map.103 = (f32[1,512]{1,0:T(1,128)S(1)}, bf16[10,512]{1,0:T(8,128)(2,1)S(1)}, f32[15,512]{1,0:T(8,128)S(1)}) custom-call(s32[128,128,128]{2,1,0:T(8,128)} %pattern.1, s32[16,128]{1,0:T(8,128)S(1)} %bitcast.7, s32[16,128]{1,0:T(8,128)S(1)} %bitcast.8, s32[2048]{0:T(1024)S(1)} %copy-done.4, s32[64,128]{1,0:T(8,128)S(1)} %bitcast.6, ...), custom_call_target="tpu_custom_call" | custom-call | tf_op jit(solution)/shard_map/pallas_call | solution.py:346
  65.0 0.6 copy.14
  65.6 0.6 copy.15
  66.2 0.6 copy.16
Async XLA Ops:
  0.6 0.8 %copy-start = (s32[8192]{0:T(1024)S(1)}, s32[8192]{0:T(1024)}, u32[]{:S(2)}) copy-start(s32[8192]{0:T(1024)} %param.12) | copy-start | bytes 98308
  1.4 0.8 %copy-start.1 = (s32[10,512]{1,0:T(8,128)S(1)}, s32[10,512]{1,0:T(8,128)}, u32[]{:S(2)}) copy-start(s32[10,512]{1,0:T(8,128)} %ext_in.1) | copy-start | bytes 61444
  2.2 0.7 %copy-start.2 = (s32[2048,1]{0,1:T(1,128)S(1)}, s32[2048,1]{0,1:T(1,128)}, u32[]{:S(2)}) copy-start(s32[2048,1]{0,1:T(1,128)} %param.9) | copy-start | bytes 24580
  2.8 0.7 %copy-start.3 = (s32[2048]{0:T(1024)S(1)}, s32[2048]{0:T(1024)}, u32[]{:S(2)}) copy-start(s32[2048]{0:T(1024)} %param.11) | copy-start | bytes 24580
  3.5 0.7 %copy-start.4 = (s32[2048]{0:T(1024)S(1)}, s32[2048]{0:T(1024)}, u32[]{:S(2)}) copy-start(s32[2048]{0:T(1024)} %src_in.1) | copy-start | bytes 24580
  4.2 0.7 %copy-start.5 = (f32[512]{0:T(512)S(1)}, f32[512]{0:T(512)}, u32[]{:S(2)}) copy-start(f32[512]{0:T(512)} %param.13) | copy-start | bytes 6148
  4.9 0.7 %copy-start.6 = (f32[512]{0:T(512)S(1)}, f32[512]{0:T(512)}, u32[]{:S(2)}) copy-start(f32[512]{0:T(512)} %param.14) | copy-start | bytes 6148

commit v5 on v4

--- a/solution.py
+++ b/solution.py
@@ -181,8 +181,8 @@
 
         lax.fori_loop(0, per // 2, build, 0)
 
-    def think(t, volt, arrived):
-        volt = alpha * volt + arrived + drive[t]
+    def think(volt, arrived):
+        volt = volt + arrived
         rate = jax.nn.sigmoid(slope * (volt - threshold))
         volt = volt - reset_part * rate
         for b in range(NB):
@@ -228,7 +228,7 @@
 
     def one_step(t, carry):
         volt, arrived = carry
-        volt, rate = think(t, volt, arrived)
+        volt, rate = think(volt, arrived)
         picked = []
         for e in range(0, edges, 32):
             mine = first[pl.ds(e, 32), :]
@@ -265,8 +265,9 @@
             return carry
 
         lax.fori_loop(0, targets // 8, turn, 0)
+        ahead = alpha * volt + drive[t + 1]
         step_messages(t).wait_recv()
-        return volt, jnp.sum(inbox[t], axis=0)
+        return ahead, jnp.sum(inbox[t], axis=0)
 
     def step_messages(t):
         return pltpu.make_async_remote_copy(
@@ -280,9 +281,9 @@
 
     pl.semaphore_wait(barrier, areas - 1)
     volt, arrived = lax.fori_loop(
-        0, steps - 1, one_step, (stacked(v_init[...]), jnp.zeros((NB, BLK), jnp.float32))
+        0, steps - 1, one_step, (alpha * stacked(v_init[...]) + drive[0], jnp.zeros((NB, BLK), jnp.float32))
     )
-    volt, rate = think(steps - 1, volt, arrived)
+    volt, rate = think(volt, arrived)
     gather_lags()
 
     def share(a):
@@ -311,7 +312,7 @@
 
         return carry
 
-    lax.fori_loop(0, areas // 2, last, 0)
+    lax.fori_loop(0, areas // 2, last, 0, unroll=4)
     acts[pl.ds(steps - 1, 1), :] = side_by_side(rate)
     pend_in[share(me), :] = pend_go[share(me), :]
     volt_out[...] = side_by_side(volt)

time: 67.7 us -> 67.7 us (level)
  no operation moved by 1% of the time
where the time goes in v5:
time: 67.7 us; the launch traced here: 66.8 us
  Pallas kernels  59.4 us (88%)
  local copies, waits for them, and re-layouts  6.76 us (10%)
    pallas_call x1, Pallas kernels, body(): pl.pallas_call(functools.partial(kernel, areas, edges, steps), out_shape=...  59.4 us
    unnamed x17, local copies, waits for them, and re-layouts  6.76 us

profile of v5, /device:TPU:11, one launch (start us, length us, event | category | flops | bytes accessed | tf_op | source)
XLA Modules:
  0.0 66.8 jit_solution(9408671998497802088)
XLA Ops:
  0.6 0.0 copy-start
  0.6 0.7 %copy-done = s32[8192]{0:T(1024)S(1)} copy-done((s32[8192]{0:T(1024)S(1)}, s32[8192]{0:T(1024)}, u32[]{:S(2)}) %copy-start) | copy-done | bytes 32792
  1.4 0.0 copy-start.1
  1.4 0.8 %copy-done.1 = s32[10,512]{1,0:T(8,128)S(1)} copy-done((s32[10,512]{1,0:T(8,128)S(1)}, s32[10,512]{1,0:T(8,128)}, u32[]{:S(2)}) %copy-start.1) | copy-done | bytes 20504
  2.2 0.0 copy-start.2
  2.2 0.7 %copy-done.2 = s32[2048,1]{0,1:T(1,128)S(1)} copy-done((s32[2048,1]{0,1:T(1,128)S(1)}, s32[2048,1]{0,1:T(1,128)}, u32[]{:S(2)}) %copy-start.2) | copy-done | bytes 8216
  2.8 0.0 copy-start.3
  2.9 0.7 %copy-done.3 = s32[2048]{0:T(1024)S(1)} copy-done((s32[2048]{0:T(1024)S(1)}, s32[2048]{0:T(1024)}, u32[]{:S(2)}) %copy-start.3) | copy-done | bytes 8216
  3.5 0.0 copy-start.4
  3.5 0.7 %copy-done.4 = s32[2048]{0:T(1024)S(1)} copy-done((s32[2048]{0:T(1024)S(1)}, s32[2048]{0:T(1024)}, u32[]{:S(2)}) %copy-start.4) | copy-done | bytes 8216
  4.2 0.0 copy-start.5
  4.2 0.7 %copy-done.5 = f32[512]{0:T(512)S(1)} copy-done((f32[512]{0:T(512)S(1)}, f32[512]{0:T(512)}, u32[]{:S(2)}) %copy-start.5) | copy-done | bytes 2072
  4.9 0.0 copy-start.6
  4.9 0.7 %copy-done.6 = f32[512]{0:T(512)S(1)} copy-done((f32[512]{0:T(512)S(1)}, f32[512]{0:T(512)}, u32[]{:S(2)}) %copy-start.6) | copy-done | bytes 2072
  5.6 59.4 %shard_map.103 = (f32[1,512]{1,0:T(1,128)S(1)}, bf16[10,512]{1,0:T(8,128)(2,1)S(1)}, f32[15,512]{1,0:T(8,128)S(1)}) custom-call(s32[128,128,128]{2,1,0:T(8,128)} %pattern.1, s32[16,128]{1,0:T(8,128)S(1)} %bitcast.7, s32[16,128]{1,0:T(8,128)S(1)} %bitcast.8, s32[2048]{0:T(1024)S(1)} %copy-done.4, s32[64,128]{1,0:T(8,128)S(1)} %bitcast.6, ...), custom_call_target="tpu_custom_call" | custom-call | tf_op jit(solution)/shard_map/pallas_call | solution.py:347
  65.0 0.6 copy.14
  65.6 0.6 copy.15
  66.2 0.6 copy.16
Async XLA Ops:
  0.6 0.8 %copy-start = (s32[8192]{0:T(1024)S(1)}, s32[8192]{0:T(1024)}, u32[]{:S(2)}) copy-start(s32[8192]{0:T(1024)} %param.12) | copy-start | bytes 98308
  1.4 0.8 %copy-start.1 = (s32[10,512]{1,0:T(8,128)S(1)}, s32[10,512]{1,0:T(8,128)}, u32[]{:S(2)}) copy-start(s32[10,512]{1,0:T(8,128)} %ext_in.1) | copy-start | bytes 61444
  2.2 0.7 %copy-start.2 = (s32[2048,1]{0,1:T(1,128)S(1)}, s32[2048,1]{0,1:T(1,128)}, u32[]{:S(2)}) copy-start(s32[2048,1]{0,1:T(1,128)} %param.9) | copy-start | bytes 24580
  2.8 0.7 %copy-start.3 = (s32[2048]{0:T(1024)S(1)}, s32[2048]{0:T(1024)}, u32[]{:S(2)}) copy-start(s32[2048]{0:T(1024)} %param.11) | copy-start | bytes 24580
  3.5 0.7 %copy-start.4 = (s32[2048]{0:T(1024)S(1)}, s32[2048]{0:T(1024)}, u32[]{:S(2)}) copy-start(s32[2048]{0:T(1024)} %src_in.1) | copy-start | bytes 24580
  4.2 0.7 %copy-start.5 = (f32[512]{0:T(512)S(1)}, f32[512]{0:T(512)}, u32[]{:S(2)}) copy-start(f32[512]{0:T(512)} %param.13) | copy-start | bytes 6148
  4.9 0.7 %copy-start.6 = (f32[512]{0:T(512)S(1)}, f32[512]{0:T(512)}, u32[]{:S(2)}) copy-start(f32[512]{0:T(512)} %param.14) | copy-start | bytes 6148
